TPU v7x, 32 devices: a whole 2x2x4 slice. The times are simulated.
32 devices in a mesh: gz: 2 (over y), gy: 4 (over x, core), gx: 4 (over z).
Axes of the slice: x: 2, y: 2, z: 4, core: 2. Of those that a mesh axis runs over, the one named last changes fastest.
Arguments:
- labels: int32 [2, 32, 512], P('gz', 'gy', 'gx'), may hold values from 0 to 7
- tissue_tensors: float32 [6, 8], replicated, as said below
- electrodes: int32 [2, 64], replicated, may hold values from 0 to 32767, as said below
- initial: float32 [64, 2, 32, 512], P(None, 'gz', 'gy', 'gx'), may hold values from -4 to 4
Outputs:
- solution: float32 [64, 2, 32, 512], P(None, 'gz', 'gy', 'gx')
- residual: float32 [64, 2, 32, 512], P(None, 'gz', 'gy', 'gx')
Inputs may be any that keep to these rules, and one draw needn't show every extreme that they name: `tissue_tensors`: the tensors are symmetric and positive definite: each off-diagonal component is at most 0.3 times the geometric mean of its two diagonal components. `electrodes`: all 128 voxel indices are distinct; voxel (z, y, x) has index (z * 32 + y) * 512 + x.
All inputs are finite; a program needn't handle non-finite values.
Results may differ from a plain program's by a relative error of at most 0.0003.
Values sent between devices are 32-bit elements; how exact they have to be, the bound alone decides.
A program may use at most 64 MiB of HBM per device.

v0:
```python
import jax
import jax.numpy as jnp
from jax import lax
from jax.sharding import PartitionSpec as P

ITERS = 2


def from_behind(value, axis, steps):
    count = lax.axis_size(axis)
    initial, last = (max(0, -steps), min(count, count - steps))
    return lax.ppermute(value, axis, [(source, source + steps) for source in range(initial, last)])


def padded_2(block, sides, width):
    for axis, dim in sides:
        count = lax.axis_size(axis)
        forward = [(i, i + 1) for i in range(count - 1)]
        backward = [(target, source) for source, target in forward]
        low = lax.ppermute(
            lax.slice_in_dim(block, block.shape[dim] - width, None, axis=dim), axis, forward
        )
        high = lax.ppermute(lax.slice_in_dim(block, 0, width, axis=dim), axis, backward)
        block = jnp.concatenate([low, block, high], axis=dim)
    return block


def tensor_lookup(labels, table):
    result = jnp.zeros((6,) + labels.shape, jnp.float32)
    for tissue in range(table.shape[1]):
        result = result + jnp.where(
            labels[None] == tissue, table[:, tissue][:, None, None, None], jnp.float32(0.0)
        )
    return result


def flux_terms(tensor, grad_x, grad_y, grad_z):
    flux_x = tensor[0] * grad_x + tensor[3] * grad_y + tensor[4] * grad_z
    flux_y = tensor[3] * grad_x + tensor[1] * grad_y + tensor[5] * grad_z
    flux_z = tensor[4] * grad_x + tensor[5] * grad_y + tensor[2] * grad_z
    return (flux_x, flux_y, flux_z)


def lower_box(tensor):
    below_z = from_behind(tensor, "gz", 1)
    below_y = from_behind(tensor[:, :, -1:], "gy", 1)
    below_x = from_behind(tensor[:, :, :, -1:], "gx", 1)
    inner = jnp.concatenate([below_x, tensor], axis=3)
    side_y = jnp.pad(below_y, ((0, 0), (0, 0), (0, 0), (1, 0)))
    inner = jnp.concatenate([side_y, inner], axis=2)
    side_z = jnp.pad(below_z, ((0, 0), (0, 0), (1, 0), (1, 0)))
    return jnp.concatenate([side_z, inner], axis=1)


def operate_faces(direction, tensor_box):
    padded = padded_2(direction, (("gz", 1), ("gy", 2), ("gx", 3)), 1)
    centre = padded[:, :-1, :-1, :-1]
    grad_z = padded[:, 1:, :-1, :-1] - centre
    grad_y = padded[:, :-1, 1:, :-1] - centre
    grad_x = padded[:, :-1, :-1, 1:] - centre
    flux_x, flux_y, flux_z = flux_terms(tensor_box, grad_x, grad_y, grad_z)
    return (
        flux_z[:, :-1, 1:, 1:]
        - flux_z[:, 1:, 1:, 1:]
        + (flux_y[:, 1:, :-1, 1:] - flux_y[:, 1:, 1:, 1:])
        + (flux_x[:, 1:, 1:, :-1] - flux_x[:, 1:, 1:, 1:])
    )


def gram_of(first, second):
    leads = first.shape[0]
    return lax.dot_general(
        first.reshape(leads, -1),
        second.reshape(leads, -1),
        (((1,), (1,)), ((), ())),
        precision=lax.Precision.HIGHEST,
        preferred_element_type=jnp.float32,
    )


def combine_rows(coef, field):
    leads = field.shape[0]
    return jnp.dot(
        coef.T,
        field.reshape(leads, -1),
        precision=lax.Precision.HIGHEST,
        preferred_element_type=jnp.float32,
    ).reshape(field.shape)


def factor_solve(matrix, target):
    factor = jnp.linalg.cholesky(matrix)
    halfway = lax.linalg.triangular_solve(factor, target, left_side=True, lower=True)
    return lax.linalg.triangular_solve(
        factor, halfway, left_side=True, lower=True, transpose_a=True
    )


def body(labels, tissue_tensors, electrodes, initial):
    cells_z, cells_y, cells_x = labels.shape
    rows_all = cells_y * lax.axis_size("gy")
    cols_all = cells_x * lax.axis_size("gx")
    depth_ids = lax.axis_index("gz") * cells_z + lax.broadcasted_iota(jnp.int32, labels.shape, 0)
    row_ids = lax.axis_index("gy") * cells_y + lax.broadcasted_iota(jnp.int32, labels.shape, 1)
    col_ids = lax.axis_index("gx") * cells_x + lax.broadcasted_iota(jnp.int32, labels.shape, 2)
    voxel_id = (depth_ids * rows_all + row_ids) * cols_all + col_ids
    sources = (voxel_id[None] == electrodes[0][:, None, None, None]).astype(jnp.float32) - (
        voxel_id[None] == electrodes[1][:, None, None, None]
    ).astype(jnp.float32)
    tensor = tensor_lookup(labels, tissue_tensors)
    tensor_box = lower_box(tensor)

    def operate(field):
        return operate_faces(field, tensor_box)

    solution = initial
    residual = sources - operate(initial)
    direction = residual
    rr_now = lax.psum(gram_of(residual, residual), ("gz", "gy", "gx"))
    for iteration in range(ITERS):
        image = operate(direction)
        curve = lax.psum(gram_of(direction, image), ("gz", "gy", "gx"))
        step_coef = factor_solve(curve, rr_now)
        solution = solution + combine_rows(step_coef, direction)
        residual = residual - combine_rows(step_coef, image)
        if iteration + 1 < ITERS:
            rr_next = lax.psum(gram_of(residual, residual), ("gz", "gy", "gx"))
            beta_coef = factor_solve(rr_now, rr_next)
            direction = residual + combine_rows(beta_coef, direction)
            rr_now = rr_next
    return (solution, residual)


def solution(mesh):
    placed = (P("gz", "gy", "gx"), P(), P(), P(None, "gz", "gy", "gx"))
    return jax.shard_map(
        body,
        mesh=mesh,
        in_specs=placed,
        out_specs=(P(None, "gz", "gy", "gx"), P(None, "gz", "gy", "gx")),
        check_vma=False,
    )
```

profile of v0, /device:TPU:0, one launch (start us, length us, event | category | flops | bytes accessed | tf_op | source)
XLA Modules:
  0.0 279.7 jit_solution(1200948065979888118)
XLA Ops:
  0.6 1.1 copy.64
  1.7 4.9 %collective-permute-start.3 = (f32[64,1,8,128]{3,0,2,1:T(8,128)S(1)}, f32[64,1,8,128]{3,0,2,1:T(8,128)S(1)}, u32[]{:S(2)}, u32[]{:S(2)}) collective-permute-start(f32[64,1,8,128]{3,0,2,1:T(8,128)S(1)} %copy.64), channel_id=1, source_target_pairs={{0,16},{1,17},{2,18},{3,19},{4,20},{5,21},{6,22},{7,23},{8,24},{9,... | collective-permute-start | bytes 786440 | tf_op jit(solution)/shard_map/ppermute | solution.py:20
  6.6 1.3 collective-permute-start.4
  7.9 0.7 compare_bitcast_fusion.7
  8.6 1.3 slice_reduce_fusion.7
  10.0 4.6 %collective-permute-start = (f32[6,1,8,128]{3,2,1,0:T(8,128)S(1)}, f32[6,1,8,128]{3,2,1,0:T(8,128)S(1)}, u32[]{:S(2)}, u32[]{:S(2)}) collective-permute-start(f32[6,1,8,128]{3,2,1,0:T(8,128)S(1)} %select_add_fusion), channel_id=1, source_target_pairs={{0,16},{1,17},{2,18},{3,19},{4,20},{5,21},{6,22},{7,23},{8,24},{9,... | collective-permute-start | bytes 73736 | tf_op jit(solution)/shard_map/ppermute | solution.py:12
  14.6 3.5 %collective-permute-start.2 = (f32[6,1,8,1]{3,2,1,0:T(8,128)S(1)}, f32[6,1,8,1]{3,2,1,0:T(8,128)S(1)}, u32[]{:S(2)}, u32[]{:S(2)}) collective-permute-start(f32[6,1,8,1]{3,2,1,0:T(8,128)S(1)} %slice.282), channel_id=1, source_target_pairs={{0,1},{1,2},{2,3},{4,5},{5,6},{6,7},{8,9},{9,10},{10,11},{12,13},{... | collective-permute-start | bytes 584 | tf_op jit(solution)/shard_map/ppermute | solution.py:12
  18.1 1.3 collective-permute-start.1
  19.5 0.8 slice_bitcast_fusion.7
  20.4 4.1 %collective-permute-start.5 = (f32[64,3,1,128]{3,0,2,1:T(8,128)S(1)}, f32[64,3,1,128]{3,0,2,1:T(8,128)S(1)}, u32[]{:S(2)}, u32[]{:S(2)}) collective-permute-start(f32[64,3,1,128]{3,0,2,1:T(8,128)S(1)} %get-tuple-element.43), channel_id=1, source_target_pairs={{0,4},{4,8},{8,12},{1,5},{5,9},{9,13},{2,6},{6,10},{10,14},{3,7},{... | collective-permute-start | bytes 294920 | tf_op jit(solution)/shard_map/ppermute | solution.py:20
  24.6 1.3 collective-permute-start.6
  26.1 1.7 collective-permute-done.6
  28.2 1.0 copy.52
  29.2 3.5 %collective-permute-start.8 = (f32[64,3,10,1]{0,3,2,1:T(1,128)}, f32[64,3,10,1]{0,3,2,1:T(1,128)S(1)}, u32[]{:S(2)}, u32[]{:S(2)}) collective-permute-start(f32[64,3,10,1]{0,3,2,1:T(1,128)} %copy.52), channel_id=1, source_target_pairs={{0,1},{1,2},{2,3},{4,5},{5,6},{6,7},{8,9},{9,10},{10,11},{12,13},{... | collective-permute-start | bytes 23048 | tf_op jit(solution)/shard_map/ppermute | solution.py:20
  33.6 1.3 collective-permute-start.7
  34.9 1.3 copy.53
  36.3 1.8 maximum_maximum_fusion
  38.1 1.2 collective-permute-done.7
  39.3 1.3 copy.51
  40.6 1.5 multiply_add_fusion.8
  43.2 1.3 collective-permute-start.10
  44.5 4.6 %collective-permute-start.9 = (f32[64,1,8,128]{3,0,2,1:T(8,128)S(1)}, f32[64,1,8,128]{3,0,2,1:T(8,128)S(1)}, u32[]{:S(2)}, u32[]{:S(2)}) collective-permute-start(f32[64,1,8,128]{3,0,2,1:T(8,128)S(1)} %fusion.21), channel_id=1, source_target_pairs={{0,16},{1,17},{2,18},{3,19},{4,20},{5,21},{6,22},{7,23},{8,24},{9,... | collective-permute-start | bytes 786440 | tf_op jit(solution)/shard_map/ppermute | solution.py:20
  49.1 4.9 %collective-permute-done.10 = f32[64,1,8,128]{3,0,2,1:T(8,128)S(1)} collective-permute-done((f32[64,1,8,128]{3,0,2,1:T(8,128)S(1)}, f32[64,1,8,128]{3,0,2,1:T(8,128)S(1)}, u32[]{:S(2)}, u32[]{:S(2)}) %collective-permute-start.10) | collective-permute-done | bytes 262176 | tf_op jit(solution)/shard_map/ppermute | solution.py:23
  54.0 1.7 collective-permute-done.9
  55.7 2.2 collective-permute-start.11
  57.9 1.3 collective-permute-start.12
  59.2 1.9 collective-permute-done.12
  61.8 3.4 %collective-permute-start.14 = (f32[64,3,10,1]{0,3,2,1:T(1,128)S(1)}, f32[64,3,10,1]{0,3,2,1:T(1,128)S(1)}, u32[]{:S(2)}, u32[]{:S(2)}) collective-permute-start(f32[64,3,10,1]{0,3,2,1:T(1,128)S(1)} %copy.56), channel_id=1, source_target_pairs={{0,1},{1,2},{2,3},{4,5},{5,6},{6,7},{8,9},{9,10},{10,11},{12,13},{... | collective-permute-start | bytes 23048 | tf_op jit(solution)/shard_map/ppermute | solution.py:20
  65.3 1.0 convolution_bitcast_fusion.10
  66.4 1.0 copy.54
  67.3 1.3 collective-permute-start.13
  68.6 1.3 copy.57
  70.0 1.8 maximum_maximum_fusion.1
  71.8 1.5 collective-permute-done.13
  73.3 2.0 copy.55
  75.3 1.5 multiply_add_fusion.5
  76.9 0.7 multiply_add_fusion.4
  78.5 42.6 %all-reduce.2 = (f32[64,64]{0,1:T(8,128)S(1)}, f32[64,64]{0,1:T(8,128)S(1)}) all-reduce(f32[64,64]{0,1:T(8,128)S(1)} %copy-done.22, f32[64,64]{0,1:T(8,128)S(1)} %convolution_bitcast_fusion.11), channel_id=1, replica_groups=mesh['gz'=2,'gy'=4,'gx'=4] {'gz','gy','gx'}, use_global_device_ids=true, to_apply=%region_3.5 | all-reduce | flops 8192 | bytes 65536 | tf_op jit(solution)/shard_map/psum | solution.py:119
  121.3 5.8 %cholesky.70 = f32[64,64]{1,0:T(8,128)S(1)} custom-call(f32[64,64]{1,0:T(8,128)S(1)} %get-tuple-element.61), custom_call_target="Cholesky" | custom-call | tf_op jit(solution)/shard_map/jit(cholesky)/cholesky | solution.py:92
  128.5 4.9 %custom-call.15 = f32[1,64,64]{1,2,0:T(8,128)S(1)} custom-call(f32[1,64,64]{2,1,0:T(8,128)S(1)} %fusion.34), custom_call_target="InvertDiagBlocksLowerTriangular" | custom-call | tf_op jit(solution)/shard_map/triangular_solve/custom-call.2 | solution.py:94
  133.4 5.9 %cholesky.59 = f32[64,64]{1,0:T(8,128)S(1)} custom-call(f32[64,64]{1,0:T(8,128)S(1)} %get-tuple-element.62), custom_call_target="Cholesky" | custom-call | tf_op jit(solution)/shard_map/jit(cholesky)/cholesky | solution.py:92
  140.6 4.9 %custom-call.13 = f32[1,64,64]{1,2,0:T(8,128)S(1)} custom-call(f32[1,64,64]{2,1,0:T(8,128)S(1)} %fusion.33), custom_call_target="InvertDiagBlocksLowerTriangular" | custom-call | tf_op jit(solution)/shard_map/triangular_solve/custom-call.2 | solution.py:94
  146.8 38.9 %psum.30 = f32[64,64]{1,0:T(8,128)S(1)} all-reduce(f32[64,64]{1,0:T(8,128)S(1)} %convolution_bitcast_fusion.9), channel_id=1, replica_groups=mesh['gz'=2,'gy'=4,'gx'=4] {'gz','gy','gx'}, use_global_device_ids=true, to_apply=%region_4.8 | all-reduce | flops 4096 | bytes 32768 | tf_op jit(solution)/shard_map/psum | solution.py:127
  186.6 4.2 %collective-permute-start.15 = (f32[64,1,8,128]{3,0,2,1:T(8,128)S(1)}, f32[64,1,8,128]{3,0,2,1:T(8,128)S(1)}, u32[]{:S(2)}, u32[]{:S(2)}) collective-permute-start(f32[64,1,8,128]{3,0,2,1:T(8,128)S(1)} %fusion.6), channel_id=1, source_target_pairs={{0,16},{1,17},{2,18},{3,19},{4,20},{5,21},{6,22},{7,23},{8,24},{9,... | collective-permute-start | bytes 786440 | tf_op jit(solution)/shard_map/ppermute | solution.py:20
  190.9 1.3 collective-permute-start.16
  192.2 3.9 %collective-permute-done.15 = f32[64,1,8,128]{3,0,2,1:T(8,128)S(1)} collective-permute-done((f32[64,1,8,128]{3,0,2,1:T(8,128)S(1)}, f32[64,1,8,128]{3,0,2,1:T(8,128)S(1)}, u32[]{:S(2)}, u32[]{:S(2)}) %collective-permute-start.15) | collective-permute-done | bytes 262176 | tf_op jit(solution)/shard_map/ppermute | solution.py:20
  196.0 4.1 %collective-permute-done.16 = f32[64,1,8,128]{3,0,2,1:T(8,128)S(1)} collective-permute-done((f32[64,1,8,128]{3,0,2,1:T(8,128)S(1)}, f32[64,1,8,128]{3,0,2,1:T(8,128)S(1)}, u32[]{:S(2)}, u32[]{:S(2)}) %collective-permute-start.16) | collective-permute-done | bytes 262176 | tf_op jit(solution)/shard_map/ppermute | solution.py:23
  200.2 1.3 collective-permute-start.17
  201.5 1.3 collective-permute-start.18
  202.8 2.9 %collective-permute-done.18 = f32[64,3,1,128]{3,0,2,1:T(8,128)S(1)} collective-permute-done((f32[64,3,1,128]{3,0,2,1:T(8,128)S(1)}, f32[64,3,1,128]{3,0,2,1:T(8,128)S(1)}, u32[]{:S(2)}, u32[]{:S(2)}) %collective-permute-start.18) | collective-permute-done | bytes 98336 | tf_op jit(solution)/shard_map/ppermute | solution.py:23
  207.2 3.3 %collective-permute-start.20 = (f32[64,3,10,1]{0,3,2,1:T(1,128)S(1)}, f32[64,3,10,1]{0,3,2,1:T(1,128)S(1)}, u32[]{:S(2)}, u32[]{:S(2)}) collective-permute-start(f32[64,3,10,1]{0,3,2,1:T(1,128)S(1)} %copy.73), channel_id=1, source_target_pairs={{0,1},{1,2},{2,3},{4,5},{5,6},{6,7},{8,9},{9,10},{10,11},{12,13},{... | collective-permute-start | bytes 23048 | tf_op jit(solution)/shard_map/ppermute | solution.py:20
  210.5 0.9 copy.77
  211.4 0.9 copy.71
  212.3 1.3 collective-permute-start.19
  213.6 1.3 copy.74
  214.9 1.9 maximum_maximum_fusion.2
  216.8 1.4 collective-permute-done.19
  218.2 2.0 copy.72
  220.3 1.6 multiply_add_fusion.2
  223.5 40.5 %psum.31 = f32[64,64]{0,1:T(8,128)S(1)} all-reduce(f32[64,64]{0,1:T(8,128)S(1)} %convolution_bitcast_fusion.8), channel_id=1, replica_groups=mesh['gz'=2,'gy'=4,'gx'=4] {'gz','gy','gx'}, use_global_device_ids=true, to_apply=%region_5.9 | all-reduce | flops 4096 | bytes 32768 | tf_op jit(solution)/shard_map/psum | solution.py:122
  264.1 5.8 %cholesky.81 = f32[64,64]{1,0:T(8,128)S(1)} custom-call(f32[64,64]{1,0:T(8,128)S(1)} %fusion.39), custom_call_target="Cholesky" | custom-call | tf_op jit(solution)/shard_map/jit(cholesky)/cholesky | solution.py:92
  271.3 4.9 %custom-call.17 = f32[1,64,64]{1,2,0:T(8,128)S(1)} custom-call(f32[1,64,64]{2,1,0:T(8,128)S(1)} %fusion.35), custom_call_target="InvertDiagBlocksLowerTriangular" | custom-call | tf_op jit(solution)/shard_map/triangular_solve/custom-call.2 | solution.py:94
  277.1 0.9 copy.84
  278.8 0.9 copy.83
  (116 shorter events, 16.1 us)
Async XLA Ops:
  0.6 19.7 %copy-start = (f32[64,1,8,128]{3,2,1,0:T(8,128)S(1)}, f32[64,1,8,128]{3,2,1,0:T(8,128)}, u32[]{:S(2)}) copy-start(f32[64,1,8,128]{3,2,1,0:T(8,128)} %param.12) | copy-start | bytes 786436
  1.7 18.6 %collective-permute-start.3 = (f32[64,1,8,128]{3,0,2,1:T(8,128)S(1)}, f32[64,1,8,128]{3,0,2,1:T(8,128)S(1)}, u32[]{:S(2)}, u32[]{:S(2)}) collective-permute-start(f32[64,1,8,128]{3,0,2,1:T(8,128)S(1)} %copy.64), channel_id=1, source_target_pairs={{0,16},{1,17},{2,18},{3,19},{4,20},{5,21},{6,22},{7,23},{8,24},{9,... | collective-permute-start | bytes 786440 | tf_op jit(solution)/shard_map/ppermute | solution.py:20
  6.6 13.8 %collective-permute-start.4 = (f32[64,1,8,128]{3,0,2,1:T(8,128)S(1)}, f32[64,1,8,128]{3,0,2,1:T(8,128)S(1)}, u32[]{:S(2)}, u32[]{:S(2)}) collective-permute-start(f32[64,1,8,128]{3,0,2,1:T(8,128)S(1)} %copy.64), channel_id=1, source_target_pairs={{16,0},{17,1},{18,2},{19,3},{20,4},{21,5},{22,6},{23,7},{24,8},{25... | collective-permute-start | bytes 786440 | tf_op jit(solution)/shard_map/ppermute | solution.py:23
  10.0 15.9 %collective-permute-start = (f32[6,1,8,128]{3,2,1,0:T(8,128)S(1)}, f32[6,1,8,128]{3,2,1,0:T(8,128)S(1)}, u32[]{:S(2)}, u32[]{:S(2)}) collective-permute-start(f32[6,1,8,128]{3,2,1,0:T(8,128)S(1)} %select_add_fusion), channel_id=1, source_target_pairs={{0,16},{1,17},{2,18},{3,19},{4,20},{5,21},{6,22},{7,23},{8,24},{9,... | collective-permute-start | bytes 73736 | tf_op jit(solution)/shard_map/ppermute | solution.py:12
  14.6 11.2 %collective-permute-start.2 = (f32[6,1,8,1]{3,2,1,0:T(8,128)S(1)}, f32[6,1,8,1]{3,2,1,0:T(8,128)S(1)}, u32[]{:S(2)}, u32[]{:S(2)}) collective-permute-start(f32[6,1,8,1]{3,2,1,0:T(8,128)S(1)} %slice.282), channel_id=1, source_target_pairs={{0,1},{1,2},{2,3},{4,5},{5,6},{6,7},{8,9},{9,10},{10,11},{12,13},{... | collective-permute-start | bytes 584 | tf_op jit(solution)/shard_map/ppermute | solution.py:12
  18.1 7.8 %collective-permute-start.1 = (f32[6,1,1,128]{3,2,1,0:T(1,128)S(1)}, f32[6,1,1,128]{3,2,1,0:T(1,128)S(1)}, u32[]{:S(2)}, u32[]{:S(2)}) collective-permute-start(f32[6,1,1,128]{3,2,1,0:T(1,128)S(1)} %slice.281), channel_id=1, source_target_pairs={{0,4},{4,8},{8,12},{1,5},{5,9},{9,13},{2,6},{6,10},{10,14},{3,7},{... | collective-permute-start | bytes 9224 | tf_op jit(solution)/shard_map/ppermute | solution.py:12
  20.4 5.6 %collective-permute-start.5 = (f32[64,3,1,128]{3,0,2,1:T(8,128)S(1)}, f32[64,3,1,128]{3,0,2,1:T(8,128)S(1)}, u32[]{:S(2)}, u32[]{:S(2)}) collective-permute-start(f32[64,3,1,128]{3,0,2,1:T(8,128)S(1)} %get-tuple-element.43), channel_id=1, source_target_pairs={{0,4},{4,8},{8,12},{1,5},{5,9},{9,13},{2,6},{6,10},{10,14},{3,7},{... | collective-permute-start | bytes 294920 | tf_op jit(solution)/shard_map/ppermute | solution.py:20
  24.6 3.2 %collective-permute-start.6 = (f32[64,3,1,128]{3,0,2,1:T(8,128)S(1)}, f32[64,3,1,128]{3,0,2,1:T(8,128)S(1)}, u32[]{:S(2)}, u32[]{:S(2)}) collective-permute-start(f32[64,3,1,128]{3,0,2,1:T(8,128)S(1)} %get-tuple-element.44), channel_id=1, source_target_pairs={{4,0},{8,4},{12,8},{5,1},{9,5},{13,9},{6,2},{10,6},{14,10},{7,3},{... | collective-permute-start | bytes 294920 | tf_op jit(solution)/shard_map/ppermute | solution.py:23
  29.2 5.8 %collective-permute-start.8 = (f32[64,3,10,1]{0,3,2,1:T(1,128)}, f32[64,3,10,1]{0,3,2,1:T(1,128)S(1)}, u32[]{:S(2)}, u32[]{:S(2)}) collective-permute-start(f32[64,3,10,1]{0,3,2,1:T(1,128)} %copy.52), channel_id=1, source_target_pairs={{0,1},{1,2},{2,3},{4,5},{5,6},{6,7},{8,9},{9,10},{10,11},{12,13},{... | collective-permute-start | bytes 23048 | tf_op jit(solution)/shard_map/ppermute | solution.py:20
  33.3 8.8 %copy-start.8 = (f32[2,9,129]{2,1,0:T(8,128)}, f32[2,9,129]{2,1,0:T(8,128)S(1)}, u32[]{:S(2)}) copy-start(f32[2,9,129]{2,1,0:T(8,128)S(1)} %get-tuple-element.45) | copy-start | bytes 27868
  33.3 8.8 %copy-start.11 = (f32[2,9,129]{2,1,0:T(8,128)}, f32[2,9,129]{2,1,0:T(8,128)S(1)}, u32[]{:S(2)}) copy-start(f32[2,9,129]{2,1,0:T(8,128)S(1)} %get-tuple-element.46) | copy-start | bytes 27868
  33.3 43.5 %copy-start.1 = (f32[2,9,129]{2,1,0:T(8,128)}, f32[2,9,129]{2,1,0:T(8,128)S(1)}, u32[]{:S(2)}) copy-start(f32[2,9,129]{2,1,0:T(8,128)S(1)} %get-tuple-element.49) | copy-start | bytes 27868
  33.3 43.5 %copy-start.3 = (f32[2,9,129]{2,1,0:T(8,128)}, f32[2,9,129]{2,1,0:T(8,128)S(1)}, u32[]{:S(2)}) copy-start(f32[2,9,129]{2,1,0:T(8,128)S(1)} %get-tuple-element.50) | copy-start | bytes 27868
  33.6 5.6 %collective-permute-start.7 = (f32[64,3,10,1]{0,3,2,1:T(1,128)S(1)}, f32[64,3,10,1]{0,3,2,1:T(1,128)S(1)}, u32[]{:S(2)}, u32[]{:S(2)}) collective-permute-start(f32[64,3,10,1]{0,3,2,1:T(1,128)S(1)} %copy.50), channel_id=1, source_target_pairs={{1,0},{2,1},{3,2},{5,4},{6,5},{7,6},{9,8},{10,9},{11,10},{13,12},{... | collective-permute-start | bytes 23048 | tf_op jit(solution)/shard_map/ppermute | solution.py:23
  36.3 4.3 %copy-start.17 = (f32[2,9,129]{2,1,0:T(8,128)S(1)}, f32[2,9,129]{2,1,0:T(8,128)}, u32[]{:S(2)}) copy-start(f32[2,9,129]{2,1,0:T(8,128)} %get-tuple-element.48) | copy-start | bytes 27868
  40.6 1.5 copy-start.14
  43.2 10.8 %collective-permute-start.10 = (f32[64,1,8,128]{3,0,2,1:T(8,128)S(1)}, f32[64,1,8,128]{3,0,2,1:T(8,128)S(1)}, u32[]{:S(2)}, u32[]{:S(2)}) collective-permute-start(f32[64,1,8,128]{3,0,2,1:T(8,128)S(1)} %fusion.21), channel_id=1, source_target_pairs={{16,0},{17,1},{18,2},{19,3},{20,4},{21,5},{22,6},{23,7},{24,8},{25... | collective-permute-start | bytes 786440 | tf_op jit(solution)/shard_map/ppermute | solution.py:23
  44.5 11.2 %collective-permute-start.9 = (f32[64,1,8,128]{3,0,2,1:T(8,128)S(1)}, f32[64,1,8,128]{3,0,2,1:T(8,128)S(1)}, u32[]{:S(2)}, u32[]{:S(2)}) collective-permute-start(f32[64,1,8,128]{3,0,2,1:T(8,128)S(1)} %fusion.21), channel_id=1, source_target_pairs={{0,16},{1,17},{2,18},{3,19},{4,20},{5,21},{6,22},{7,23},{8,24},{9,... | collective-permute-start | bytes 786440 | tf_op jit(solution)/shard_map/ppermute | solution.py:20
  55.7 3.5 %collective-permute-start.11 = (f32[64,3,1,128]{3,0,2,1:T(8,128)S(1)}, f32[64,3,1,128]{3,0,2,1:T(8,128)S(1)}, u32[]{:S(2)}, u32[]{:S(2)}) collective-permute-start(f32[64,3,1,128]{3,0,2,1:T(8,128)S(1)} %get-tuple-element.41), channel_id=1, source_target_pairs={{0,4},{4,8},{8,12},{1,5},{5,9},{9,13},{2,6},{6,10},{10,14},{3,7},{... | collective-permute-start | bytes 294920 | tf_op jit(solution)/shard_map/ppermute | solution.py:20
  57.9 3.2 %collective-permute-start.12 = (f32[64,3,1,128]{3,0,2,1:T(8,128)S(1)}, f32[64,3,1,128]{3,0,2,1:T(8,128)S(1)}, u32[]{:S(2)}, u32[]{:S(2)}) collective-permute-start(f32[64,3,1,128]{3,0,2,1:T(8,128)S(1)} %get-tuple-element.42), channel_id=1, source_target_pairs={{4,0},{8,4},{12,8},{5,1},{9,5},{13,9},{6,2},{10,6},{14,10},{7,3},{... | collective-permute-start | bytes 294920 | tf_op jit(solution)/shard_map/ppermute | solution.py:23
  61.8 6.8 %collective-permute-start.14 = (f32[64,3,10,1]{0,3,2,1:T(1,128)S(1)}, f32[64,3,10,1]{0,3,2,1:T(1,128)S(1)}, u32[]{:S(2)}, u32[]{:S(2)}) collective-permute-start(f32[64,3,10,1]{0,3,2,1:T(1,128)S(1)} %copy.56), channel_id=1, source_target_pairs={{0,1},{1,2},{2,3},{4,5},{5,6},{6,7},{8,9},{9,10},{10,11},{12,13},{... | collective-permute-start | bytes 23048 | tf_op jit(solution)/shard_map/ppermute | solution.py:20
  67.3 5.9 %collective-permute-start.13 = (f32[64,3,10,1]{0,3,2,1:T(1,128)}, f32[64,3,10,1]{0,3,2,1:T(1,128)}, u32[]{:S(2)}, u32[]{:S(2)}) collective-permute-start(f32[64,3,10,1]{0,3,2,1:T(1,128)} %copy.54), channel_id=1, source_target_pairs={{1,0},{2,1},{3,2},{5,4},{6,5},{7,6},{9,8},{10,9},{11,10},{13,12},{... | collective-permute-start | bytes 23048 | tf_op jit(solution)/shard_map/ppermute | solution.py:23
  75.3 1.5 copy-start.9
  75.3 1.5 copy-start.12
  75.3 1.5 copy-start.15
  77.5 1.0 copy-start.22
  146.0 40.7 %copy-start.18 = (f32[64,64,1]{0,1,2:T(8,128)}, f32[64,64,1]{0,1,2:T(8,128)S(1)}, u32[]{:S(2)}) copy-start(f32[64,64,1]{0,1,2:T(8,128)S(1)} %convolution_bitcast_fusion.7) | copy-start | bytes 49156
  185.6 0.6 copy-start.20
  186.6 9.4 %collective-permute-start.15 = (f32[64,1,8,128]{3,0,2,1:T(8,128)S(1)}, f32[64,1,8,128]{3,0,2,1:T(8,128)S(1)}, u32[]{:S(2)}, u32[]{:S(2)}) collective-permute-start(f32[64,1,8,128]{3,0,2,1:T(8,128)S(1)} %fusion.6), channel_id=1, source_target_pairs={{0,16},{1,17},{2,18},{3,19},{4,20},{5,21},{6,22},{7,23},{8,24},{9,... | collective-permute-start | bytes 786440 | tf_op jit(solution)/shard_map/ppermute | solution.py:20
  190.9 9.3 %collective-permute-start.16 = (f32[64,1,8,128]{3,0,2,1:T(8,128)S(1)}, f32[64,1,8,128]{3,0,2,1:T(8,128)S(1)}, u32[]{:S(2)}, u32[]{:S(2)}) collective-permute-start(f32[64,1,8,128]{3,0,2,1:T(8,128)S(1)} %fusion.6), channel_id=1, source_target_pairs={{16,0},{17,1},{18,2},{19,3},{20,4},{21,5},{22,6},{23,7},{24,8},{25... | collective-permute-start | bytes 786440 | tf_op jit(solution)/shard_map/ppermute | solution.py:23
  200.2 2.6 collective-permute-start.17
  201.5 4.3 %collective-permute-start.18 = (f32[64,3,1,128]{3,0,2,1:T(8,128)S(1)}, f32[64,3,1,128]{3,0,2,1:T(8,128)S(1)}, u32[]{:S(2)}, u32[]{:S(2)}) collective-permute-start(f32[64,3,1,128]{3,0,2,1:T(8,128)S(1)} %get-tuple-element.40), channel_id=1, source_target_pairs={{4,0},{8,4},{12,8},{5,1},{9,5},{13,9},{6,2},{10,6},{14,10},{7,3},{... | collective-permute-start | bytes 294920 | tf_op jit(solution)/shard_map/ppermute | solution.py:23
  202.8 2.9 %copy-start.6 = (f32[64,3,1,128]{3,0,2,1:T(8,128)}, f32[64,3,1,128]{3,0,2,1:T(8,128)S(1)}, u32[]{:S(2)}) copy-start(f32[64,3,1,128]{3,0,2,1:T(8,128)S(1)} %collective-permute-done.17) | copy-start | bytes 294916
  205.7 0.6 copy-start.7
  207.2 6.4 %collective-permute-start.20 = (f32[64,3,10,1]{0,3,2,1:T(1,128)S(1)}, f32[64,3,10,1]{0,3,2,1:T(1,128)S(1)}, u32[]{:S(2)}, u32[]{:S(2)}) collective-permute-start(f32[64,3,10,1]{0,3,2,1:T(1,128)S(1)} %copy.73), channel_id=1, source_target_pairs={{0,1},{1,2},{2,3},{4,5},{5,6},{6,7},{8,9},{9,10},{10,11},{12,13},{... | collective-permute-start | bytes 23048 | tf_op jit(solution)/shard_map/ppermute | solution.py:20
  212.3 5.9 %collective-permute-start.19 = (f32[64,3,10,1]{0,3,2,1:T(1,128)}, f32[64,3,10,1]{0,3,2,1:T(1,128)}, u32[]{:S(2)}, u32[]{:S(2)}) collective-permute-start(f32[64,3,10,1]{0,3,2,1:T(1,128)} %copy.71), channel_id=1, source_target_pairs={{1,0},{2,1},{3,2},{5,4},{6,5},{7,6},{9,8},{10,9},{11,10},{13,12},{... | collective-permute-start | bytes 23048 | tf_op jit(solution)/shard_map/ppermute | solution.py:23
  220.3 1.6 copy-start.2
  220.3 1.6 copy-start.4
  220.3 1.6 copy-start.10
  220.3 1.6 copy-start.13
  220.3 1.6 copy-start.16
  222.6 53.6 %copy-start.21 = (f32[64,64]{1,0:T(8,128)S(1)}, f32[64,64]{1,0:T(8,128)}, u32[]{:S(2)}) copy-start(f32[64,64]{1,0:T(8,128)} %copy-done.20) | copy-start | bytes 49156
  223.4 54.6 %copy-start.5 = (f32[64,1,8,128]{3,2,0,1:T(8,128)S(1)}, f32[64,1,8,128]{3,2,0,1:T(8,128)}, u32[]{:S(2)}) copy-start(f32[64,1,8,128]{3,2,0,1:T(8,128)} %copy.77) | copy-start | bytes 786436
  264.0 14.4 %copy-start.19 = (f32[64,64,1]{0,1,2:T(8,128)S(1)}, f32[64,64,1]{0,1,2:T(8,128)}, u32[]{:S(2)}) copy-start(f32[64,64,1]{0,1,2:T(8,128)} %copy-done.18) | copy-start | bytes 49156
where the time goes:
time: 281 us; the launch traced here: 280 us
  blocking collectives  122 us (43%)
  starting transfers between devices  52.4 us (19%)
  other arithmetic  50.7 us (18%)
  waiting for transfers between devices  25.3 us (9%)
  local copies, waits for them, and re-layouts  22.4 us (8%)
  matrix products  5.49 us (2%)
    psum x1, blocking collectives, body(): rr_now = lax.psum(gram_of(residual, residual), ('gz', 'gy', 'gx'))  42.6 us
    psum x1, blocking collectives, body(): curve = lax.psum(gram_of(direction, image), ('gz', 'gy', 'gx'))  40.5 us
    psum x1, blocking collectives, body(): rr_next = lax.psum(gram_of(residual, residual), ('gz', 'gy', 'gx'))  38.9 us
    ppermute x9, starting transfers between devices, padded_2(): lax.ppermute(lax.slice_in_dim(block, block.shape[dim] - width, None, axis...  31.5 us
    ppermute x9, waiting for transfers between devices, padded_2(): lax.ppermute(lax.slice_in_dim(block, 0, width, axis=dim), axis, backward)  19.7 us
    another operation x9, other arithmetic, factor_solve(): factor = jnp.linalg.cholesky(matrix)  19.6 us
    another operation x6, other arithmetic, factor_solve(): lax.linalg.triangular_solve(factor, halfway, left_side=True, lower=True,...  16.6 us
    ppermute x9, starting transfers between devices, padded_2(): lax.ppermute(lax.slice_in_dim(block, 0, width, axis=dim), axis, backward)  11.6 us
  transfers between devices with their start and end apart: 21, of which 10 were waited for; matrix products, arithmetic and copies ran while one was open for 6% of the time, Pallas kernels for 0%

commit v1 on v0

--- a/solution.py
+++ b/solution.py
@@ -116,7 +116,9 @@
     solution = initial
     residual = sources - operate(initial)
     direction = residual
-    rr_now = lax.psum(gram_of(residual, residual), ("gz", "gy", "gx"))
+    x = gram_of(residual, residual)
+    parts = lax.all_gather(x, ("gz", "gy", "gx"))
+    rr_now = jnp.sum(parts, axis=0)
     for iteration in range(ITERS):
         image = operate(direction)
         curve = lax.psum(gram_of(direction, image), ("gz", "gy", "gx"))

time: 281 us -> 343 us (1.22)
  blocking collectives: 122 us -> 194 us
  waiting for transfers between devices: 25.3 us -> 17.5 us
    all_gather x0 -> x1, blocking collectives: none -> 74.6 us  [body(): parts = lax.all_gather(x, ('gz', 'gy', 'gx'))]
    psum x1 -> x0, blocking collectives: 42.6 us -> none  [body(): rr_now = lax.psum(gram_of(residual, residual), ('gz', 'gy', 'gx'))]
    psum x1 -> x2, blocking collectives: 40.5 us -> 79.6 us  [body(): curve = lax.psum(gram_of(direction, image), ('gz', 'gy', 'gx'))]
    ppermute x9, waiting for transfers between devices: 19.7 us -> 14.2 us  [padded_2(): lax.ppermute(lax.slice_in_dim(block, 0, width, axis=dim), axis, backward)]
  transfers between devices with their start and end apart: 21 -> 21, of which waited for: 10 -> 8; matrix products, arithmetic and copies ran while one was open for 6% -> 9% of each run, Pallas kernels for 0% -> 0%
where the time goes in v1:
time: 343 us; the launch traced here: 341 us
  blocking collectives  194 us (57%)
  other arithmetic  51.5 us (15%)
  starting transfers between devices  49.7 us (14%)
  local copies, waits for them, and re-layouts  22.4 us (7%)
  waiting for transfers between devices  17.5 us (5%)
  matrix products  4.85 us (1%)
    psum x2, blocking collectives, body(): curve = lax.psum(gram_of(direction, image), ('gz', 'gy', 'gx'))  79.6 us
    all_gather x1, blocking collectives, body(): parts = lax.all_gather(x, ('gz', 'gy', 'gx'))  74.6 us
    psum x1, blocking collectives, body(): rr_next = lax.psum(gram_of(residual, residual), ('gz', 'gy', 'gx'))  39.8 us
    ppermute x9, starting transfers between devices, padded_2(): lax.ppermute(lax.slice_in_dim(block, block.shape[dim] - width, None, axis...  28.8 us
    another operation x9, other arithmetic, factor_solve(): factor = jnp.linalg.cholesky(matrix)  19.6 us
    another operation x6, other arithmetic, factor_solve(): lax.linalg.triangular_solve(factor, halfway, left_side=True, lower=True,...  17.3 us
    ppermute x9, waiting for transfers between devices, padded_2(): lax.ppermute(lax.slice_in_dim(block, 0, width, axis=dim), axis, backward)  14.2 us
    ppermute x9, starting transfers between devices, padded_2(): lax.ppermute(lax.slice_in_dim(block, 0, width, axis=dim), axis, backward)  11.6 us
  transfers between devices with their start and end apart: 21, of which 8 were waited for; matrix products, arithmetic and copies ran while one was open for 9% of the time, Pallas kernels for 0%

profile of v1, /device:TPU:0, one launch (start us, length us, event | category | flops | bytes accessed | tf_op | source)
XLA Modules:
  0.0 341.4 jit_solution(13187715406471645363)
XLA Ops:
  0.6 1.1 copy.61
  1.7 4.9 %collective-permute-start.3 = (f32[64,1,8,128]{3,0,2,1:T(8,128)S(1)}, f32[64,1,8,128]{3,0,2,1:T(8,128)S(1)}, u32[]{:S(2)}, u32[]{:S(2)}) collective-permute-start(f32[64,1,8,128]{3,0,2,1:T(8,128)S(1)} %copy.61), channel_id=1, source_target_pairs={{0,16},{1,17},{2,18},{3,19},{4,20},{5,21},{6,22},{7,23},{8,24},{9,... | collective-permute-start | bytes 786440 | tf_op jit(solution)/shard_map/ppermute | solution.py:20
  6.6 1.3 collective-permute-start.4
  7.9 0.7 compare_bitcast_fusion.7
  8.6 1.3 slice_reduce_fusion.7
  10.0 4.6 %collective-permute-start = (f32[6,1,8,128]{3,2,1,0:T(8,128)S(1)}, f32[6,1,8,128]{3,2,1,0:T(8,128)S(1)}, u32[]{:S(2)}, u32[]{:S(2)}) collective-permute-start(f32[6,1,8,128]{3,2,1,0:T(8,128)S(1)} %select_add_fusion), channel_id=1, source_target_pairs={{0,16},{1,17},{2,18},{3,19},{4,20},{5,21},{6,22},{7,23},{8,24},{9,... | collective-permute-start | bytes 73736 | tf_op jit(solution)/shard_map/ppermute | solution.py:12
  14.6 3.5 %collective-permute-start.2 = (f32[6,1,8,1]{3,2,1,0:T(8,128)S(1)}, f32[6,1,8,1]{3,2,1,0:T(8,128)S(1)}, u32[]{:S(2)}, u32[]{:S(2)}) collective-permute-start(f32[6,1,8,1]{3,2,1,0:T(8,128)S(1)} %slice.282), channel_id=1, source_target_pairs={{0,1},{1,2},{2,3},{4,5},{5,6},{6,7},{8,9},{9,10},{10,11},{12,13},{... | collective-permute-start | bytes 584 | tf_op jit(solution)/shard_map/ppermute | solution.py:12
  18.1 1.3 collective-permute-start.1
  19.5 0.8 slice_bitcast_fusion.7
  20.4 4.1 %collective-permute-start.5 = (f32[64,3,1,128]{3,0,2,1:T(8,128)S(1)}, f32[64,3,1,128]{3,0,2,1:T(8,128)S(1)}, u32[]{:S(2)}, u32[]{:S(2)}) collective-permute-start(f32[64,3,1,128]{3,0,2,1:T(8,128)S(1)} %get-tuple-element.41), channel_id=1, source_target_pairs={{0,4},{4,8},{8,12},{1,5},{5,9},{9,13},{2,6},{6,10},{10,14},{3,7},{... | collective-permute-start | bytes 294920 | tf_op jit(solution)/shard_map/ppermute | solution.py:20
  24.6 1.3 collective-permute-start.6
  26.1 1.7 collective-permute-done.6
  28.2 1.0 copy.50
  29.2 3.5 %collective-permute-start.8 = (f32[64,3,10,1]{0,3,2,1:T(1,128)}, f32[64,3,10,1]{0,3,2,1:T(1,128)S(1)}, u32[]{:S(2)}, u32[]{:S(2)}) collective-permute-start(f32[64,3,10,1]{0,3,2,1:T(1,128)} %copy.50), channel_id=1, source_target_pairs={{0,1},{1,2},{2,3},{4,5},{5,6},{6,7},{8,9},{9,10},{10,11},{12,13},{... | collective-permute-start | bytes 23048 | tf_op jit(solution)/shard_map/ppermute | solution.py:20
  33.6 1.3 collective-permute-start.7
  35.0 1.3 copy.51
  36.3 1.8 maximum_maximum_fusion
  38.1 1.2 collective-permute-done.7
  39.3 1.3 copy.49
  40.6 1.5 multiply_add_fusion.8
  43.6 1.3 collective-permute-start.10
  44.9 4.6 %collective-permute-start.9 = (f32[64,1,8,128]{3,0,2,1:T(8,128)S(1)}, f32[64,1,8,128]{3,0,2,1:T(8,128)S(1)}, u32[]{:S(2)}, u32[]{:S(2)}) collective-permute-start(f32[64,1,8,128]{3,0,2,1:T(8,128)S(1)} %fusion.21), channel_id=1, source_target_pairs={{0,16},{1,17},{2,18},{3,19},{4,20},{5,21},{6,22},{7,23},{8,24},{9,... | collective-permute-start | bytes 786440 | tf_op jit(solution)/shard_map/ppermute | solution.py:20
  49.5 74.6 %all-gather = f32[2048,64]{1,0:T(8,128)S(1)} all-gather(f32[64,64]{1,0:T(8,128)S(1)} %convolution_bitcast_fusion.10), channel_id=2, replica_groups=mesh['gz'=2,'gy'=4,'gx'=4] {'gz','gy','gx'}, dimensions={0}, use_global_device_ids=true | all-gather | bytes 540672 | tf_op jit(solution)/shard_map/all_gather | solution.py:120
  124.2 5.8 %cholesky.70 = f32[64,64]{1,0:T(8,128)S(1)} custom-call(f32[64,64]{1,0:T(8,128)S(1)} %fusion.43), custom_call_target="Cholesky" | custom-call | tf_op jit(solution)/shard_map/jit(cholesky)/cholesky | solution.py:92
  130.1 1.3 collective-permute-start.11
  131.4 1.3 collective-permute-start.12
  133.4 1.3 collective-permute-done.12
  135.4 1.9 collective-permute-start.14
  138.2 5.5 %custom-call.15 = f32[1,64,64]{1,2,0:T(8,128)} custom-call(f32[1,64,64]{2,1,0:T(8,128)S(1)} %fusion.34), custom_call_target="InvertDiagBlocksLowerTriangular" | custom-call | tf_op jit(solution)/shard_map/triangular_solve/custom-call.2 | solution.py:94
  143.7 1.0 copy.52
  144.6 1.3 collective-permute-start.13
  145.9 1.3 copy.55
  147.3 1.8 maximum_maximum_fusion.1
  149.0 1.5 collective-permute-done.13
  150.6 2.0 copy.53
  152.6 1.5 multiply_add_fusion.5
  154.2 0.7 multiply_add_fusion.4
  155.8 39.2 %psum.21 = f32[64,64]{0,1:T(8,128)S(1)} all-reduce(f32[64,64]{0,1:T(8,128)S(1)} %convolution_bitcast_fusion.11), channel_id=1, replica_groups=mesh['gz'=2,'gy'=4,'gx'=4] {'gz','gy','gx'}, use_global_device_ids=true, to_apply=%region_0.1 | all-reduce | flops 4096 | bytes 32768 | tf_op jit(solution)/shard_map/psum | solution.py:124
  195.1 5.8 %cholesky.59 = f32[64,64]{1,0:T(8,128)S(1)} custom-call(f32[64,64]{1,0:T(8,128)S(1)} %fusion.47), custom_call_target="Cholesky" | custom-call | tf_op jit(solution)/shard_map/jit(cholesky)/cholesky | solution.py:92
  200.9 0.7 compare_reduce_fusion.2
  201.7 0.7 fusion.33
  202.4 4.9 %custom-call.13 = f32[1,64,64]{1,2,0:T(8,128)S(1)} custom-call(f32[1,64,64]{2,1,0:T(8,128)S(1)} %fusion.33), custom_call_target="InvertDiagBlocksLowerTriangular" | custom-call | tf_op jit(solution)/shard_map/triangular_solve/custom-call.2 | solution.py:94
  208.5 39.8 %psum.22 = f32[64,64]{1,0:T(8,128)S(1)} all-reduce(f32[64,64]{1,0:T(8,128)S(1)} %convolution_bitcast_fusion.9), channel_id=1, replica_groups=mesh['gz'=2,'gy'=4,'gx'=4] {'gz','gy','gx'}, use_global_device_ids=true, to_apply=%region_4.8 | all-reduce | flops 4096 | bytes 32768 | tf_op jit(solution)/shard_map/psum | solution.py:129
  249.3 4.2 %collective-permute-start.15 = (f32[64,1,8,128]{3,0,2,1:T(8,128)S(1)}, f32[64,1,8,128]{3,0,2,1:T(8,128)S(1)}, u32[]{:S(2)}, u32[]{:S(2)}) collective-permute-start(f32[64,1,8,128]{3,0,2,1:T(8,128)S(1)} %fusion.6), channel_id=1, source_target_pairs={{0,16},{1,17},{2,18},{3,19},{4,20},{5,21},{6,22},{7,23},{8,24},{9,... | collective-permute-start | bytes 786440 | tf_op jit(solution)/shard_map/ppermute | solution.py:20
  253.6 1.3 collective-permute-start.16
  254.9 3.3 collective-permute-done.15
  258.2 4.1 %collective-permute-done.16 = f32[64,1,8,128]{3,0,2,1:T(8,128)S(1)} collective-permute-done((f32[64,1,8,128]{3,0,2,1:T(8,128)S(1)}, f32[64,1,8,128]{3,0,2,1:T(8,128)S(1)}, u32[]{:S(2)}, u32[]{:S(2)}) %collective-permute-start.16) | collective-permute-done | bytes 262176 | tf_op jit(solution)/shard_map/ppermute | solution.py:23
  262.3 1.3 collective-permute-start.17
  263.6 1.3 collective-permute-start.18
  264.9 2.9 collective-permute-done.18
  269.3 3.0 collective-permute-start.20
  272.3 0.9 copy.74
  273.2 0.9 copy.68
  274.1 1.3 collective-permute-start.19
  275.4 1.3 copy.71
  276.8 1.9 maximum_maximum_fusion.2
  278.6 1.4 collective-permute-done.19
  280.1 2.0 copy.69
  282.1 1.6 multiply_add_fusion.2
  285.4 40.4 %psum.23 = f32[64,64]{0,1:T(8,128)S(1)} all-reduce(f32[64,64]{0,1:T(8,128)S(1)} %convolution_bitcast_fusion.8), channel_id=1, replica_groups=mesh['gz'=2,'gy'=4,'gx'=4] {'gz','gy','gx'}, use_global_device_ids=true, to_apply=%region_5.9 | all-reduce | flops 4096 | bytes 32768 | tf_op jit(solution)/shard_map/psum | solution.py:124
  325.9 5.8 %cholesky.81 = f32[64,64]{1,0:T(8,128)S(1)} custom-call(f32[64,64]{1,0:T(8,128)S(1)} %fusion.39), custom_call_target="Cholesky" | custom-call | tf_op jit(solution)/shard_map/jit(cholesky)/cholesky | solution.py:92
  333.1 4.9 %custom-call.17 = f32[1,64,64]{1,2,0:T(8,128)S(1)} custom-call(f32[1,64,64]{2,1,0:T(8,128)S(1)} %fusion.35), custom_call_target="InvertDiagBlocksLowerTriangular" | custom-call | tf_op jit(solution)/shard_map/triangular_solve/custom-call.2 | solution.py:94
  338.9 0.9 copy.81
  340.6 0.9 copy.80
  (123 shorter events, 15.3 us)
Async XLA Ops:
  0.6 19.7 %copy-start = (f32[64,1,8,128]{3,2,1,0:T(8,128)S(1)}, f32[64,1,8,128]{3,2,1,0:T(8,128)}, u32[]{:S(2)}) copy-start(f32[64,1,8,128]{3,2,1,0:T(8,128)} %param.12) | copy-start | bytes 786436
  1.7 18.6 %collective-permute-start.3 = (f32[64,1,8,128]{3,0,2,1:T(8,128)S(1)}, f32[64,1,8,128]{3,0,2,1:T(8,128)S(1)}, u32[]{:S(2)}, u32[]{:S(2)}) collective-permute-start(f32[64,1,8,128]{3,0,2,1:T(8,128)S(1)} %copy.61), channel_id=1, source_target_pairs={{0,16},{1,17},{2,18},{3,19},{4,20},{5,21},{6,22},{7,23},{8,24},{9,... | collective-permute-start | bytes 786440 | tf_op jit(solution)/shard_map/ppermute | solution.py:20
  6.6 13.8 %collective-permute-start.4 = (f32[64,1,8,128]{3,0,2,1:T(8,128)S(1)}, f32[64,1,8,128]{3,0,2,1:T(8,128)S(1)}, u32[]{:S(2)}, u32[]{:S(2)}) collective-permute-start(f32[64,1,8,128]{3,0,2,1:T(8,128)S(1)} %copy.61), channel_id=1, source_target_pairs={{16,0},{17,1},{18,2},{19,3},{20,4},{21,5},{22,6},{23,7},{24,8},{25... | collective-permute-start | bytes 786440 | tf_op jit(solution)/shard_map/ppermute | solution.py:23
  10.0 15.9 %collective-permute-start = (f32[6,1,8,128]{3,2,1,0:T(8,128)S(1)}, f32[6,1,8,128]{3,2,1,0:T(8,128)S(1)}, u32[]{:S(2)}, u32[]{:S(2)}) collective-permute-start(f32[6,1,8,128]{3,2,1,0:T(8,128)S(1)} %select_add_fusion), channel_id=1, source_target_pairs={{0,16},{1,17},{2,18},{3,19},{4,20},{5,21},{6,22},{7,23},{8,24},{9,... | collective-permute-start | bytes 73736 | tf_op jit(solution)/shard_map/ppermute | solution.py:12
  14.6 11.2 %collective-permute-start.2 = (f32[6,1,8,1]{3,2,1,0:T(8,128)S(1)}, f32[6,1,8,1]{3,2,1,0:T(8,128)S(1)}, u32[]{:S(2)}, u32[]{:S(2)}) collective-permute-start(f32[6,1,8,1]{3,2,1,0:T(8,128)S(1)} %slice.282), channel_id=1, source_target_pairs={{0,1},{1,2},{2,3},{4,5},{5,6},{6,7},{8,9},{9,10},{10,11},{12,13},{... | collective-permute-start | bytes 584 | tf_op jit(solution)/shard_map/ppermute | solution.py:12
  18.1 7.8 %collective-permute-start.1 = (f32[6,1,1,128]{3,2,1,0:T(1,128)S(1)}, f32[6,1,1,128]{3,2,1,0:T(1,128)S(1)}, u32[]{:S(2)}, u32[]{:S(2)}) collective-permute-start(f32[6,1,1,128]{3,2,1,0:T(1,128)S(1)} %slice.281), channel_id=1, source_target_pairs={{0,4},{4,8},{8,12},{1,5},{5,9},{9,13},{2,6},{6,10},{10,14},{3,7},{... | collective-permute-start | bytes 9224 | tf_op jit(solution)/shard_map/ppermute | solution.py:12
  20.4 5.6 %collective-permute-start.5 = (f32[64,3,1,128]{3,0,2,1:T(8,128)S(1)}, f32[64,3,1,128]{3,0,2,1:T(8,128)S(1)}, u32[]{:S(2)}, u32[]{:S(2)}) collective-permute-start(f32[64,3,1,128]{3,0,2,1:T(8,128)S(1)} %get-tuple-element.41), channel_id=1, source_target_pairs={{0,4},{4,8},{8,12},{1,5},{5,9},{9,13},{2,6},{6,10},{10,14},{3,7},{... | collective-permute-start | bytes 294920 | tf_op jit(solution)/shard_map/ppermute | solution.py:20
  24.6 3.2 collective-permute-start.6
  29.2 5.8 %collective-permute-start.8 = (f32[64,3,10,1]{0,3,2,1:T(1,128)}, f32[64,3,10,1]{0,3,2,1:T(1,128)S(1)}, u32[]{:S(2)}, u32[]{:S(2)}) collective-permute-start(f32[64,3,10,1]{0,3,2,1:T(1,128)} %copy.50), channel_id=1, source_target_pairs={{0,1},{1,2},{2,3},{4,5},{5,6},{6,7},{8,9},{9,10},{10,11},{12,13},{... | collective-permute-start | bytes 23048 | tf_op jit(solution)/shard_map/ppermute | solution.py:20
  33.3 8.8 %copy-start.8 = (f32[2,9,129]{2,1,0:T(8,128)}, f32[2,9,129]{2,1,0:T(8,128)S(1)}, u32[]{:S(2)}) copy-start(f32[2,9,129]{2,1,0:T(8,128)S(1)} %get-tuple-element.43) | copy-start | bytes 27868
  33.3 8.8 %copy-start.11 = (f32[2,9,129]{2,1,0:T(8,128)}, f32[2,9,129]{2,1,0:T(8,128)S(1)}, u32[]{:S(2)}) copy-start(f32[2,9,129]{2,1,0:T(8,128)S(1)} %get-tuple-element.44) | copy-start | bytes 27868
  33.3 120.8 %copy-start.1 = (f32[2,9,129]{2,1,0:T(8,128)}, f32[2,9,129]{2,1,0:T(8,128)S(1)}, u32[]{:S(2)}) copy-start(f32[2,9,129]{2,1,0:T(8,128)S(1)} %get-tuple-element.47) | copy-start | bytes 27868
  33.3 120.8 %copy-start.3 = (f32[2,9,129]{2,1,0:T(8,128)}, f32[2,9,129]{2,1,0:T(8,128)S(1)}, u32[]{:S(2)}) copy-start(f32[2,9,129]{2,1,0:T(8,128)S(1)} %get-tuple-element.48) | copy-start | bytes 27868
  33.6 5.6 %collective-permute-start.7 = (f32[64,3,10,1]{0,3,2,1:T(1,128)S(1)}, f32[64,3,10,1]{0,3,2,1:T(1,128)S(1)}, u32[]{:S(2)}, u32[]{:S(2)}) collective-permute-start(f32[64,3,10,1]{0,3,2,1:T(1,128)S(1)} %copy.48), channel_id=1, source_target_pairs={{1,0},{2,1},{3,2},{5,4},{6,5},{7,6},{9,8},{10,9},{11,10},{13,12},{... | collective-permute-start | bytes 23048 | tf_op jit(solution)/shard_map/ppermute | solution.py:23
  36.3 4.3 %copy-start.17 = (f32[2,9,129]{2,1,0:T(8,128)S(1)}, f32[2,9,129]{2,1,0:T(8,128)}, u32[]{:S(2)}) copy-start(f32[2,9,129]{2,1,0:T(8,128)} %get-tuple-element.46) | copy-start | bytes 27868
  40.6 1.5 copy-start.14
  43.6 86.5 %collective-permute-start.10 = (f32[64,1,8,128]{3,0,2,1:T(8,128)S(1)}, f32[64,1,8,128]{3,0,2,1:T(8,128)S(1)}, u32[]{:S(2)}, u32[]{:S(2)}) collective-permute-start(f32[64,1,8,128]{3,0,2,1:T(8,128)S(1)} %fusion.21), channel_id=1, source_target_pairs={{16,0},{17,1},{18,2},{19,3},{20,4},{21,5},{22,6},{23,7},{24,8},{25... | collective-permute-start | bytes 786440 | tf_op jit(solution)/shard_map/ppermute | solution.py:23
  44.9 85.2 %collective-permute-start.9 = (f32[64,1,8,128]{3,0,2,1:T(8,128)S(1)}, f32[64,1,8,128]{3,0,2,1:T(8,128)S(1)}, u32[]{:S(2)}, u32[]{:S(2)}) collective-permute-start(f32[64,1,8,128]{3,0,2,1:T(8,128)S(1)} %fusion.21), channel_id=1, source_target_pairs={{0,16},{1,17},{2,18},{3,19},{4,20},{5,21},{6,22},{7,23},{8,24},{9,... | collective-permute-start | bytes 786440 | tf_op jit(solution)/shard_map/ppermute | solution.py:20
  124.1 6.0 %copy-start.18 = (f32[64,64]{1,0:T(8,128)}, f32[64,64]{1,0:T(8,128)S(1)}, u32[]{:S(2)}) copy-start(f32[64,64]{1,0:T(8,128)S(1)} %reduce_sum.9) | copy-start | bytes 49156
  130.1 3.2 collective-permute-start.11
  131.4 3.2 collective-permute-start.12
  135.4 10.5 %collective-permute-start.14 = (f32[64,3,10,1]{0,3,2,1:T(1,128)S(1)}, f32[64,3,10,1]{0,3,2,1:T(1,128)S(1)}, u32[]{:S(2)}, u32[]{:S(2)}) collective-permute-start(f32[64,3,10,1]{0,3,2,1:T(1,128)S(1)} %copy.54), channel_id=1, source_target_pairs={{0,1},{1,2},{2,3},{4,5},{5,6},{6,7},{8,9},{9,10},{10,11},{12,13},{... | collective-permute-start | bytes 23048 | tf_op jit(solution)/shard_map/ppermute | solution.py:20
  144.6 5.9 %collective-permute-start.13 = (f32[64,3,10,1]{0,3,2,1:T(1,128)}, f32[64,3,10,1]{0,3,2,1:T(1,128)}, u32[]{:S(2)}, u32[]{:S(2)}) collective-permute-start(f32[64,3,10,1]{0,3,2,1:T(1,128)} %copy.52), channel_id=1, source_target_pairs={{1,0},{2,1},{3,2},{5,4},{6,5},{7,6},{9,8},{10,9},{11,10},{13,12},{... | collective-permute-start | bytes 23048 | tf_op jit(solution)/shard_map/ppermute | solution.py:23
  152.6 1.5 copy-start.9
  152.6 1.5 copy-start.12
  152.6 1.5 copy-start.15
  154.8 52.4 %copy-start.19 = (f32[64,64]{1,0:T(8,128)S(1)}, f32[64,64]{1,0:T(8,128)}, u32[]{:S(2)}) copy-start(f32[64,64]{1,0:T(8,128)} %copy-done.18) | copy-start | bytes 49156
  155.6 92.7 %copy-start.24 = (f32[1,64,64]{1,2,0:T(8,128)S(1)}, f32[1,64,64]{1,2,0:T(8,128)}, u32[]{:S(2)}) copy-start(f32[1,64,64]{1,2,0:T(8,128)} %custom-call.15) | copy-start | bytes 49156
  207.8 41.6 %copy-start.20 = (f32[64,64,1]{0,1,2:T(8,128)}, f32[64,64,1]{0,1,2:T(8,128)S(1)}, u32[]{:S(2)}) copy-start(f32[64,64,1]{0,1,2:T(8,128)S(1)} %convolution_bitcast_fusion.7) | copy-start | bytes 49156
  248.3 0.6 copy-start.22
  249.3 8.8 %collective-permute-start.15 = (f32[64,1,8,128]{3,0,2,1:T(8,128)S(1)}, f32[64,1,8,128]{3,0,2,1:T(8,128)S(1)}, u32[]{:S(2)}, u32[]{:S(2)}) collective-permute-start(f32[64,1,8,128]{3,0,2,1:T(8,128)S(1)} %fusion.6), channel_id=1, source_target_pairs={{0,16},{1,17},{2,18},{3,19},{4,20},{5,21},{6,22},{7,23},{8,24},{9,... | collective-permute-start | bytes 786440 | tf_op jit(solution)/shard_map/ppermute | solution.py:20
  253.6 8.7 %collective-permute-start.16 = (f32[64,1,8,128]{3,0,2,1:T(8,128)S(1)}, f32[64,1,8,128]{3,0,2,1:T(8,128)S(1)}, u32[]{:S(2)}, u32[]{:S(2)}) collective-permute-start(f32[64,1,8,128]{3,0,2,1:T(8,128)S(1)} %fusion.6), channel_id=1, source_target_pairs={{16,0},{17,1},{18,2},{19,3},{20,4},{21,5},{22,6},{23,7},{24,8},{25... | collective-permute-start | bytes 786440 | tf_op jit(solution)/shard_map/ppermute | solution.py:23
  262.3 2.6 collective-permute-start.17
  263.6 4.3 %collective-permute-start.18 = (f32[64,3,1,128]{3,0,2,1:T(8,128)S(1)}, f32[64,3,1,128]{3,0,2,1:T(8,128)S(1)}, u32[]{:S(2)}, u32[]{:S(2)}) collective-permute-start(f32[64,3,1,128]{3,0,2,1:T(8,128)S(1)} %get-tuple-element.38), channel_id=1, source_target_pairs={{4,0},{8,4},{12,8},{5,1},{9,5},{13,9},{6,2},{10,6},{14,10},{7,3},{... | collective-permute-start | bytes 294920 | tf_op jit(solution)/shard_map/ppermute | solution.py:23
  264.9 2.9 copy-start.6
  267.9 0.6 copy-start.7
  269.3 6.2 %collective-permute-start.20 = (f32[64,3,10,1]{0,3,2,1:T(1,128)S(1)}, f32[64,3,10,1]{0,3,2,1:T(1,128)S(1)}, u32[]{:S(2)}, u32[]{:S(2)}) collective-permute-start(f32[64,3,10,1]{0,3,2,1:T(1,128)S(1)} %copy.70), channel_id=1, source_target_pairs={{0,1},{1,2},{2,3},{4,5},{5,6},{6,7},{8,9},{9,10},{10,11},{12,13},{... | collective-permute-start | bytes 23048 | tf_op jit(solution)/shard_map/ppermute | solution.py:20
  274.1 5.9 %collective-permute-start.19 = (f32[64,3,10,1]{0,3,2,1:T(1,128)}, f32[64,3,10,1]{0,3,2,1:T(1,128)}, u32[]{:S(2)}, u32[]{:S(2)}) collective-permute-start(f32[64,3,10,1]{0,3,2,1:T(1,128)} %copy.68), channel_id=1, source_target_pairs={{1,0},{2,1},{3,2},{5,4},{6,5},{7,6},{9,8},{10,9},{11,10},{13,12},{... | collective-permute-start | bytes 23048 | tf_op jit(solution)/shard_map/ppermute | solution.py:23
  282.1 1.6 copy-start.2
  282.1 1.6 copy-start.4
  282.1 1.6 copy-start.10
  282.1 1.6 copy-start.13
  282.1 1.6 copy-start.16
  284.4 53.6 %copy-start.23 = (f32[64,64]{1,0:T(8,128)S(1)}, f32[64,64]{1,0:T(8,128)}, u32[]{:S(2)}) copy-start(f32[64,64]{1,0:T(8,128)} %copy-done.22) | copy-start | bytes 49156
  285.2 54.6 %copy-start.5 = (f32[64,1,8,128]{3,2,0,1:T(8,128)S(1)}, f32[64,1,8,128]{3,2,0,1:T(8,128)}, u32[]{:S(2)}) copy-start(f32[64,1,8,128]{3,2,0,1:T(8,128)} %copy.74) | copy-start | bytes 786436
  325.8 14.4 %copy-start.21 = (f32[64,64,1]{0,1,2:T(8,128)S(1)}, f32[64,64,1]{0,1,2:T(8,128)}, u32[]{:S(2)}) copy-start(f32[64,64,1]{0,1,2:T(8,128)} %copy-done.20) | copy-start | bytes 49156
